TPU v7x, 128 devices: a whole 4x4x4 slice. The times are simulated.
128 devices in a mesh: expert: 8 (over y, core), frame: 16 (over z, x).
Axes of the slice: x: 4, y: 4, z: 4, core: 2. Of those that a mesh axis runs over, the one named last changes fastest.
Arguments:
- tokens: bfloat16 [4096, 4096], P('frame'), may hold values from -6 to 6
- routes: int32 [4096, 2], P('frame'), may hold values from 0 to 7, all different within a row; in each aligned block of 256 rows (0 to 255, 256 to 511, ...) at most 96 rows name the same one
- route_weight: float32 [4096, 2], P('frame'), may hold values from 0.2 to 1
- moe_gain: float32 [4096], replicated, may hold values from 0.1 to 1.9
- gate_weight: bfloat16 [8, 7168, 4096], P('expert', 'frame'), may hold values from -0.09375 to 0.09375
- up_weight: bfloat16 [8, 7168, 4096], P('expert', 'frame'), may hold values from -0.09375 to 0.09375
- down_weight: bfloat16 [8, 7168, 4096], P('expert', 'frame'), may hold values from -0.0625 to 0.0625
- ssd_gain: float32 [4096], replicated, may hold values from 0.1 to 1.9
- input_weight: bfloat16 [4096, 8192], P(None, 'expert'), may hold values from -0.09375 to 0.09375
- write_weight: bfloat16 [4096, 1024], P(None, 'expert'), may hold values from -0.0078125 to 0.0078125
- read_weight: bfloat16 [4096, 1024], P(None, 'expert'), may hold values from -0.0078125 to 0.0078125
- step_weight: bfloat16 [4096, 128], P(None, 'expert'), may hold values from -0.375 to 0.375
- step_bias: float32 [128], P('expert'), may hold values from -5 to -4.2
- decay_log: float32 [128], P('expert'), may hold values from -9.1 to 1.39
- skip_gain: float32 [128], P('expert'), may hold values from -3 to 3
Outputs:
- mixed: bfloat16 [4096, 4096], P('frame', 'expert')
- ssd_out: bfloat16 [4096, 8192], P('frame', 'expert')
Inputs may be any that keep to these rules, and one draw needn't show every extreme that they name: `routes`: each token names two different experts. In each aligned block of 256 tokens no expert is named by more than 96 tokens, and in every draw some expert is named by exactly 96 tokens of some block.
All inputs are finite; a program needn't handle non-finite values.
Results may differ from a plain program's by a relative error of at most 0.034.
Values may be sent and summed in bfloat16 or wider, within the bound.
No kernel may reach another device: no remote copies, remote signals or barrier semaphores. Data moves between devices by JAX's collectives and lax.ppermute only.
A program may use at most 128 MiB of HBM per device.

v0:
```python
import jax
import jax.numpy as jnp
from jax import lax
from jax.sharding import PartitionSpec as P

HEAD_DIM = 64
STATE = 128
SPAN = 128


EPSILON = 1e-06
PRECISE = lax.Precision.HIGHEST


def carried_in(x, axis, combine, identity):
    devices, mine = (lax.axis_size(axis), lax.axis_index(axis))
    everything = jax.tree.map(
        lambda part, kind: lax.all_gather(part.astype(kind), axis), x, (jnp.bfloat16, jnp.bfloat16)
    )
    start = jax.tree.map(
        lambda part, zero: jnp.broadcast_to(jnp.asarray(zero, part.dtype), part.shape), x, identity
    )

    def turn(k, before):
        reached = k < mine
        new = combine(
            before, jax.tree.map(lambda part, own: part[k].astype(own.dtype), everything, x)
        )
        return jax.tree.map(lambda a, b: jnp.where(reached, a, b), new, before)

    return lax.fori_loop(0, devices, turn, start)


def rms_scale(values, gain):
    mean_sq = jnp.mean(values * values, axis=-1, keepdims=True)
    return values * lax.rsqrt(mean_sq + EPSILON) * gain


def span_terms(span_x, span_b, span_c, span_dt, span_decay):
    cumulative = jnp.cumsum(span_decay, axis=0)
    length = span_x.shape[0]
    gaps = cumulative[:, None, :] - cumulative[None, :, :]
    causal = jnp.arange(length)[:, None] >= jnp.arange(length)[None, :]
    decays = jnp.exp(jnp.where(causal[:, :, None], gaps, -jnp.inf))
    scores = jnp.einsum("ihn,jhn->ijh", span_c, span_b, precision=PRECISE)
    mixing = scores * decays * span_dt[None, :, :]
    inside = jnp.einsum("ijh,jhp->ihp", mixing, span_x, precision=PRECISE)
    to_end = jnp.exp(cumulative[-1][None, :] - cumulative) * span_dt
    states = jnp.einsum("jh,jhn,jhp->hnp", to_end, span_b, span_x, precision=PRECISE)
    return (cumulative, inside, states)


def link_states(earlier, later):
    return (earlier[0] + later[0], jnp.exp(later[0])[:, None, None] * earlier[1] + later[1])


def body(
    tokens,
    routes,
    route_weight,
    moe_gain,
    gate_weight,
    up_weight,
    down_weight,
    ssd_gain,
    input_weight,
    write_weight,
    read_weight,
    step_weight,
    step_bias,
    decay_log,
    skip_gain,
):
    tok_rows, width = tokens.shape
    local_count = gate_weight.shape[0]
    expert_axis = lax.axis_size("expert")
    capacity = 3 * tok_rows // (local_count * expert_axis)
    normed = rms_scale(tokens.astype(jnp.float32), moe_gain).astype(jnp.bfloat16)
    expert = lax.axis_index("expert") * local_count + 0
    hits = routes == expert
    chosen = jnp.any(hits, axis=1)
    weights = jnp.sum(jnp.where(hits, route_weight, 0.0), axis=1)
    slot_index = jnp.cumsum(chosen.astype(jnp.int32)) - 1
    slot_ids = jnp.arange(capacity, dtype=jnp.int32)
    onehot = (slot_index[None, :] == slot_ids[:, None]) & chosen[None, :]
    picked = jnp.dot(
        onehot.astype(jnp.bfloat16), normed, preferred_element_type=jnp.float32
    ).astype(jnp.bfloat16)
    gate_w = gate_weight[0]
    up_w = up_weight[0]
    down_w = down_weight[0]
    piece = lax.all_gather(picked, "frame", axis=0, tiled=True)
    gate = jnp.einsum("rd,fd->rf", piece, gate_w, preferred_element_type=jnp.float32)
    upper = jnp.einsum("rd,fd->rf", piece, up_w, preferred_element_type=jnp.float32)
    hidden = (jax.nn.silu(gate) * upper).astype(jnp.bfloat16)
    returned = lax.psum_scatter(
        jnp.dot(hidden, down_w, preferred_element_type=jnp.float32).astype(jnp.bfloat16),
        "frame",
        scatter_dimension=0,
        tiled=True,
    ).astype(jnp.float32)
    placed = jnp.dot(onehot.astype(jnp.float32).T, returned, precision=PRECISE)
    weighted = weights[:, None] * placed
    col_count = width // expert_axis
    col_start = lax.axis_index("expert") * col_count
    summed = lax.psum(weighted.astype(jnp.bfloat16), "expert").astype(jnp.float32)
    mixed_full = (tokens.astype(jnp.float32) + summed).astype(jnp.bfloat16)
    ssd_in = rms_scale(mixed_full.astype(jnp.float32), ssd_gain).astype(jnp.bfloat16)
    mixed = lax.dynamic_slice_in_dim(mixed_full, col_start, col_count, 1)
    heads_dev = step_weight.shape[1]
    groups_dev = write_weight.shape[1] // STATE
    per_group = heads_dev // groups_dev
    blocks = tok_rows // SPAN
    inputs = jnp.dot(ssd_in, input_weight, preferred_element_type=jnp.float32).astype(jnp.bfloat16)
    writes = jnp.dot(ssd_in, write_weight, preferred_element_type=jnp.float32).astype(jnp.bfloat16)
    reads = jnp.dot(ssd_in, read_weight, preferred_element_type=jnp.float32).astype(jnp.bfloat16)
    step_size = jax.nn.softplus(
        jnp.dot(ssd_in, step_weight, preferred_element_type=jnp.float32) + step_bias
    )
    log_decay = -step_size * jnp.exp(decay_log)
    span_x = inputs.astype(jnp.float32).reshape(blocks, SPAN, heads_dev, HEAD_DIM)
    span_b = jnp.repeat(
        writes.astype(jnp.float32).reshape(blocks, SPAN, groups_dev, STATE), per_group, axis=2
    )
    span_c = jnp.repeat(
        reads.astype(jnp.float32).reshape(blocks, SPAN, groups_dev, STATE), per_group, axis=2
    )
    span_dt = step_size.reshape(blocks, SPAN, heads_dev)
    span_decay = log_decay.reshape(blocks, SPAN, heads_dev)
    cumulative, inside, states = jax.vmap(span_terms)(span_x, span_b, span_c, span_dt, span_decay)
    running = jnp.zeros((heads_dev, STATE, HEAD_DIM), jnp.float32)
    log_sum = jnp.zeros((heads_dev,), jnp.float32)
    starts = []
    for block in range(blocks):
        starts.append((log_sum, running))
        running = jnp.exp(cumulative[block, -1])[:, None, None] * running + states[block]
        log_sum = log_sum + cumulative[block, -1]
    prior_log, incoming = carried_in(
        (log_sum, running), "frame", link_states, (jnp.zeros_like(log_sum), jnp.zeros_like(running))
    )
    pieces = []
    for block in range(blocks):
        before_log, before_state = starts[block]
        carried = jnp.exp(before_log)[:, None, None] * incoming + before_state
        from_prior = jnp.exp(cumulative[block])[:, :, None] * jnp.einsum(
            "ihn,hnp->ihp", span_c[block], carried, precision=PRECISE
        )
        pieces.append(inside[block] + from_prior + skip_gain[None, :, None] * span_x[block])
    ssd_out = jnp.stack(pieces).reshape(tok_rows, heads_dev * HEAD_DIM).astype(jnp.bfloat16)
    return (mixed, ssd_out)


def solution(mesh):
    placed = (
        P("frame", None),
        P("frame", None),
        P("frame", None),
        P(),
        P("expert", "frame", None),
        P("expert", "frame", None),
        P("expert", "frame", None),
        P(),
        P(None, "expert"),
        P(None, "expert"),
        P(None, "expert"),
        P(None, "expert"),
        P("expert"),
        P("expert"),
        P("expert"),
    )
    return jax.shard_map(
        body,
        mesh=mesh,
        in_specs=placed,
        out_specs=(P("frame", "expert"), P("frame", "expert")),
        check_vma=False,
    )
```

profile of v0, /device:TPU:1, one launch (start us, length us, event | category | flops | bytes accessed | tf_op | source)
XLA Modules:
  0.0 422.9 jit_solution(17950568232959835423)
XLA Ops:
  8.6 2.1 fusion.5
  10.7 3.3 convolution_convert_fusion.1
  14.1 93.5 %all-gather.4.cloned.1.call-done = bf16[1536,4096]{1,0:T(8,128)(2,1)} async-done(((bf16[96,4096]{1,0:T(8,128)(2,1)}), bf16[1536,4096]{1,0:T(8,128)(2,1)}) %all-gather.4.cloned.1.call-update) | async-done | bytes 12582928 | tf_op jit(solution)/shard_map/all_gather | solution.py:92
  107.6 11.1 %fusion.12 = f32[1536,448]{0,1:T(8,128)} fusion(bf16[1536,4096]{1,0:T(8,128)(2,1)} %all-gather.4.cloned.1.call-done, bf16[1,448,4096]{2,1,0:T(8,128)(2,1)} %param.21), kind=kOutput, calls=%fused_computation.23 | convolution fusion | flops 5637144576 | bytes 19005440 | tf_op jit(solution)/shard_map/rd,fd->rf/dot_general | solution.py:93
  118.7 24.5 %convolution_convert_fusion = bf16[1536,4096]{1,0:T(8,128)(2,1)} fusion(bf16[1,448,4096]{2,1,0:T(8,128)(2,1)} %param.23, bf16[1536,4096]{1,0:T(8,128)(2,1)} %all-gather.4.cloned.1.call-done, bf16[1,448,4096]{2,1,0:T(8,128)(2,1)} %param.22, f32[1536,448]{0,1:T(8,128)} %fusion.12), kind=kOutput, calls=%fused_computation.4 | convolution fusion | flops 11284709376 | bytes 35258368 | tf_op jit(solution)/shard_map/dot_general | solution.py:97
  143.9 93.5 %reduce-scatter.2.cloned.1.call-done = bf16[96,4096]{1,0:T(8,128)(2,1)} async-done(((bf16[1536,4096]{1,0:T(8,128)(2,1)}), bf16[96,4096]{1,0:T(8,128)(2,1)}) %reduce-scatter.2.cloned.1.call-update) | async-done | bytes 786448 | tf_op jit(solution)/shard_map/reduce_scatter | solution.py:96
  237.4 3.2 fusion.1
  240.7 63.0 %all-reduce.2.cloned.1.call-done = bf16[256,4096]{1,0:T(8,128)(2,1)} async-done(((bf16[256,4096]{1,0:T(8,128)(2,1)}), bf16[256,4096]{1,0:T(8,128)(2,1)}) %all-reduce.2.cloned.1.call-update) | async-done | bytes 2097168 | tf_op jit(solution)/shard_map/psum | solution.py:106
  303.8 2.5 fusion.2
  310.8 6.5 %convolution_convert_fusion.2 = bf16[256,1024]{1,0:T(8,128)(2,1)} fusion(bf16[256,4096]{1,0:T(8,128)(2,1)S(1)} %fusion.4, bf16[4096,1024]{1,0:T(8,128)(2,1)} %param.25), kind=kOutput, calls=%fused_computation.39 | convolution fusion | flops 2147745792 | bytes 11010048 | tf_op jit(solution)/shard_map/dot_general | solution.py:114
  317.4 2.1 copy.50
  319.4 2.0 reshape.158
  322.9 1.8 fusion.48
  326.8 17.2 %all-gather = bf16[16,1,16]{2,1,0:T(2,128)(2,1)S(1)} all-gather(bf16[1,1,16]{2,1,0:T(2,128)(2,1)S(1)} %copy-done.18), channel_id=2, replica_groups=mesh['expert'=8,'frame'=16] {'frame'}, dimensions={0}, use_global_device_ids=true | all-gather | bytes 544 | tf_op jit(solution)/shard_map/all_gather | solution.py:18
  344.9 2.1 copy.63
  348.1 1.7 constant_dynamic-slice_fusion.1
  349.8 2.6 fusion.47
  352.4 4.4 %fusion.54 = f32[2,16,128,128]{3,2,1,0:T(8,128)S(1)} fusion(f32[2,128,128]{2,1,0:T(8,128)S(1)} %bitcast.123, f32[2,128,128]{2,1,0:T(8,128)S(1)} %convert.14), kind=kOutput, calls=%fused_computation.63 | convolution fusion | flops 805306368 | bytes 2359296 | tf_op jit(solution)/shard_map/vmap(ihn,jhn->ijh)/dot_general | solution.py:45
  356.8 3.3 fusion.34
  360.1 19.9 %all-gather.6.cloned.1.call-done = bf16[16,16,128,64]{2,3,1,0:T(8,128)(2,1)} async-done(((bf16[1,16,128,64]{2,3,1,0:T(8,128)(2,1)}), bf16[16,16,128,64]{2,3,1,0:T(8,128)(2,1)}) %all-gather.6.cloned.1.call-update) | async-done | bytes 4194320 | tf_op jit(solution)/shard_map/all_gather | solution.py:18
  380.0 27.1 %while.14 = (s32[]{:T(128)}, f32[16,128,64]{2,1,0:T(8,128)S(1)}, s32[]{:T(128)}, bf16[16,16]{1,0:T(8,128)(2,1)S(1)}, bf16[16,16,128,64]{2,3,1,0:T(8,128)(2,1)}, /*index=5*/s32[]{:T(128)}, s32[]{:T(128)}) while((s32[]{:T(128)}, f32[16,128,64]{2,1,0:T(8,128)S(1)}, s32[]{:T(128)}, bf16[16,16]{1,0:T(8,128)(2,1)S(1)}, ...), condition=%wide.region_10.11_spmd.clone, body=%wide.region_9.10_spmd.clone.sunk | while | flops 655380 | bytes 2359561 | solution.py:31
  408.3 3.4 fusion.46
  411.8 2.2 fusion.45
  414.8 1.5 reshape.173
  (157 shorter events, 40.8 us)
Async XLA Ops:
  7.2 314.2 %copy-start = (bf16[4096,128]{1,0:T(8,128)(2,1)S(1)}, bf16[4096,128]{1,0:T(8,128)(2,1)}, u32[]{:S(2)}) copy-start(bf16[4096,128]{1,0:T(8,128)(2,1)} %param.26) | copy-start | bytes 3145732
  7.2 100.4 %all-gather.4.cloned.1.call-start = ((), (), s32[]{:S(2)}) async-start(), calls=%async_computation.1 | async-start | bytes 13369344 | tf_op jit(solution)/shard_map/all_gather | solution.py:92
  14.1 223.3 %reduce-scatter.2.cloned.1.call-start = ((), (), s32[]{:S(2)}) async-start(), calls=%async_computation.2 | async-start | bytes 13369344 | tf_op jit(solution)/shard_map/reduce_scatter | solution.py:96
  143.2 97.5 %copy-start.22 = (f32[16]{0:T(128)S(1)}, f32[16]{0:T(128)}, u32[]{:S(2)}) copy-start(f32[16]{0:T(128)} %param.30) | copy-start | bytes 196
  143.2 160.5 %copy-start.3 = (bf16[256,4096]{1,0:T(8,128)(2,1)S(1)}, bf16[256,4096]{1,0:T(8,128)(2,1)}, u32[]{:S(2)}) copy-start(bf16[256,4096]{1,0:T(8,128)(2,1)} %param.17) | copy-start | bytes 6291460
  143.3 160.5 %all-reduce.2.cloned.1.call-start = ((), (), s32[]{:S(2)}) async-start(), calls=%async_computation.3 | async-start | bytes 4194304 | tf_op jit(solution)/shard_map/psum | solution.py:106
  240.6 139.3 %all-gather.6.cloned.1.call-start = ((), (), s32[]{:S(2)}) async-start(), calls=%async_computation.4 | async-start | bytes 4456448 | tf_op jit(solution)/shard_map/all_gather | solution.py:18
  240.7 65.7 %copy-start.13 = (f32[4096]{0:T(1024)S(1)}, f32[4096]{0:T(1024)}, u32[]{:S(2)}) copy-start(f32[4096]{0:T(1024)} %param.24) | copy-start | bytes 49156
  306.3 1.7 copy-start.2
  306.3 1.0 copy-start.12
  307.3 14.1 %copy-start.1 = (bf16[256,4096]{1,0:T(8,128)(2,1)}, bf16[256,4096]{1,0:T(8,128)(2,1)S(1)}, u32[]{:S(2)}) copy-start(bf16[256,4096]{1,0:T(8,128)(2,1)S(1)} %fusion.4) | copy-start | bytes 6291460
  321.4 1.0 copy-start.9
  322.1 3.7 copy-start.15
  322.1 3.7 copy-start.17
  322.4 4.3 %copy-start.18 = (bf16[1,1,16]{2,1,0:T(2,128)(2,1)S(1)}, bf16[1,1,16]{2,1,0:T(2,128)(2,1)}, u32[]{:S(2)}) copy-start(bf16[1,1,16]{2,1,0:T(2,128)(2,1)} %get-tuple-element.154) | copy-start | bytes 100
  322.4 21.5 %copy-start.6 = (bf16[256,1024]{1,0:T(8,128)(2,1)S(1)}, bf16[256,1024]{1,0:T(8,128)(2,1)}, u32[]{:S(2)}) copy-start(bf16[256,1024]{1,0:T(8,128)(2,1)} %convolution_convert_fusion.2) | copy-start | bytes 1572868
  324.7 1.1 copy-start.4
  349.8 7.0 %copy-start.10 = (bf16[2,128,16,64]{1,0,3,2:T(2,128)(2,1)S(1)}, bf16[2,128,16,64]{1,0,3,2:T(2,128)(2,1)}, u32[]{:S(2)}) copy-start(bf16[2,128,16,64]{1,0,3,2:T(2,128)(2,1)} %reshape.158) | copy-start | bytes 1572868
  380.0 28.3 %copy-start.20 = (f32[16]{0:T(128)S(1)}, f32[16]{0:T(128)}, u32[]{:S(2)}) copy-start(f32[16]{0:T(128)} %param.31) | copy-start | bytes 196
  407.1 4.6 %copy-start.5 = (f32[2,16,128,64]{2,3,1,0:T(8,128)S(1)}, f32[2,16,128,64]{2,3,1,0:T(8,128)}, u32[]{:S(2)}) copy-start(f32[2,16,128,64]{2,3,1,0:T(8,128)} %copy-done.4) | copy-start | bytes 3145732
  407.1 4.6 %copy-start.16 = (f32[16]{0:T(128)S(1)}, f32[16]{0:T(128)}, u32[]{:S(2)}) copy-start(f32[16]{0:T(128)} %get-tuple-element.152) | copy-start | bytes 196
  408.3 3.4 copy-start.7
  408.3 3.4 copy-start.8
  408.3 3.4 copy-start.11
  (3 other events, 2.4 us)
Sparse Core Ops, SparseCore 0:
  14.2 93.3 all-gather.3
  143.3 93.9 reduce-scatter.1
  240.8 62.9 all-reduce.1
  326.8 53.1 all-gather.5
where the time goes:
time: 424 us; the launch traced here: 423 us
  waiting for transfers between devices  270 us (64%)
  matrix products  67.7 us (16%)
  local copies, waits for them, and re-layouts  36.7 us (9%)
  blocking collectives  17.2 us (4%)
  other arithmetic  16.3 us (4%)
  between operations  14.1 us (3%)
    reduce_scatter x1, waiting for transfers between devices, body(): lax.psum_scatter(jnp.dot(hidden, down_w, preferred_element_type=jnp.float...  93.5 us
    all_gather x1, waiting for transfers between devices, body(): piece = lax.all_gather(picked, 'frame', axis=0, tiled=True)  93.5 us
    psum x1, waiting for transfers between devices, body(): lax.psum(weighted.astype(jnp.bfloat16), 'expert').astype(jnp.float32)  63 us
    dot_general x1, matrix products, body(): jnp.dot(hidden, down_w, preferred_element_type=jnp.float32)  24.5 us
    dynamic_slice x32, local copies, waits for them, and re-layouts, turn(): part[k].astype(own.dtype)  20.1 us
    all_gather x1, waiting for transfers between devices, carried_in(): lax.all_gather(part.astype(kind), axis)  19.9 us
    all_gather x1, blocking collectives, carried_in(): lax.all_gather(part.astype(kind), axis)  17.2 us
    dot_general x1, matrix products, body(): jnp.einsum('rd,fd->rf', piece, gate_w, preferred_element_type=jnp.float32)  11.1 us
  transfers between devices with their start and end apart: 4, of which 4 were waited for; matrix products, arithmetic and copies ran while one was open for 4% of the time, Pallas kernels for 0%

commit v1 on v0

v1 whole, which is shorter than its diff:
```python
import functools

import jax
import jax.numpy as jnp
from jax import lax
from jax.experimental import pallas as pl
from jax.experimental.pallas import tpu as pltpu
from jax.sharding import PartitionSpec as P

HEAD_DIM = 64
STATE = 128
SLOTS = 96
SIDE = 4
EPSILON = 1e-06
PRECISE = lax.Precision.HIGHEST
AXES = ("expert", "frame")
VMEM_BYTES = 48 * 1024 * 1024
F32, BF16 = jnp.float32, jnp.bfloat16


def routes_of(rule):
    pairs = []
    for y in range(SIDE):
        for core in range(2):
            for z in range(SIDE):
                for x in range(SIDE):
                    ny, nc, nz, nx = rule(y, core, z, x)
                    source = (y * 2 + core) * 16 + z * SIDE + x
                    target = ((ny % SIDE) * 2 + nc % 2) * 16 + (nz % SIDE) * SIDE + nx % SIDE
                    pairs.append((source, target))
    return pairs


def send(array, rule):
    return lax.ppermute(array, AXES, routes_of(rule))


def along_first(array, by):
    return send(array, lambda y, c, z, x: (y, c, z + by * c, x + by * (1 - c)))


def along_second(array, by):
    return send(array, lambda y, c, z, x: (y, c, z + by * (1 - c), x + by * c))


def along_x(array, by):
    return send(array, lambda y, c, z, x: (y, c, z, x + by))


def along_z(array, by):
    return send(array, lambda y, c, z, x: (y, c, z + by, x))


def along_y(array, by):
    return send(array, lambda y, c, z, x: (y + by, c, z, x))


def to_sibling(array):
    return send(array, lambda y, c, z, x: (y, 1 - c, z, x))


def shape(dims, kind):
    return jax.ShapeDtypeStruct(dims, kind)


def params():
    return pltpu.CompilerParams(vmem_limit_bytes=VMEM_BYTES)


def pick_kernel(where_ref, tokens_ref, routes_ref, weight_ref, gain_ref, rows_ref, onehot_ref, slot_weight_ref):
    count = tokens_ref.shape[0]
    hits = routes_ref[...] == where_ref[0]
    chosen = jnp.max(hits.astype(F32), axis=1, keepdims=True)
    weights = jnp.sum(jnp.where(hits, weight_ref[...], 0.0), axis=1, keepdims=True)
    lower = lax.broadcasted_iota(jnp.int32, (count, count), 0) >= lax.broadcasted_iota(jnp.int32, (count, count), 1)
    wide = jnp.broadcast_to(chosen, (count, SLOTS))
    place = jnp.dot(lower.astype(BF16), wide.astype(BF16), preferred_element_type=F32) - 1.0
    slot = lax.broadcasted_iota(jnp.int32, (count, SLOTS), 1)
    onehot = jnp.where((place.astype(jnp.int32) == slot) & (wide > 0.0), 1.0, 0.0).astype(BF16)
    onehot_ref[...] = onehot
    slot_weight_ref[...] = jnp.broadcast_to(weights, slot_weight_ref.shape)
    picked = lax.dot_general(onehot, tokens_ref[...], (((0,), (0,)), ((), ())), preferred_element_type=F32)
    mean_sq = jnp.mean(picked * picked, axis=1, keepdims=True)
    rows_ref[...] = (picked * lax.rsqrt(mean_sq + EPSILON) * gain_ref[...]).astype(BF16)


def pick(where, tokens, routes, route_weight, gain):
    count, width = tokens.shape
    smem, vmem = pl.BlockSpec(memory_space=pltpu.SMEM), pl.BlockSpec(memory_space=pltpu.VMEM)
    return pl.pallas_call(
        pick_kernel,
        out_shape=(shape((SLOTS, width), BF16), shape((count, SLOTS), BF16), shape((count, 128), F32)),
        in_specs=[smem, vmem, vmem, vmem, vmem],
        out_specs=(vmem, vmem, vmem),
        compiler_params=params(),
        name="pick",
    )(where, tokens, routes, route_weight, gain.reshape(1, width))


def expert_hidden(rows, gate_w, up_w):
    gate = jnp.einsum("rd,fd->rf", rows, gate_w, preferred_element_type=F32)
    upper = jnp.einsum("rd,fd->rf", rows, up_w, preferred_element_type=F32)
    return (jax.nn.silu(gate) * upper).astype(BF16)


def expert_out(rows, gate_w, up_w, down_w):
    return jnp.dot(expert_hidden(rows, gate_w, up_w), down_w, preferred_element_type=F32).astype(BF16)


def plus(a, b):
    return (a.astype(F32) + b.astype(F32)).astype(BF16)


def experts(rows, gate_w, up_w, down_w):
    half = 2 * SLOTS
    near = jnp.concatenate([rows, along_first(rows, 1), along_first(rows, -1), along_first(rows, 2)], axis=0)
    before = along_second(near, 1)
    after = along_second(near, -1)
    far_top = along_second(before[:half], 1)
    far_bottom = along_second(after[half:], -1)
    out_near = expert_out(near, gate_w, up_w, down_w)
    out_before = expert_out(before, gate_w, up_w, down_w)
    out_after = expert_out(after, gate_w, up_w, down_w)
    far = jnp.concatenate([far_top, far_bottom], axis=0)
    out_far = expert_out(far, gate_w, up_w, down_w)
    relay_down = along_second(out_far[:half], 1)
    relay_up = along_second(out_far[half:], -1)
    to_after = jnp.concatenate([plus(out_after[:half], relay_down), out_after[half:]], axis=0)
    to_before = jnp.concatenate([out_before[:half], plus(out_before[half:], relay_up)], axis=0)
    from_before = along_second(to_after, 1)
    from_after = along_second(to_before, -1)
    total = (out_near.astype(F32) + from_before.astype(F32) + from_after.astype(F32)).astype(BF16)
    own, down, up, across = [total[k * SLOTS : (k + 1) * SLOTS] for k in range(4)]
    return own, along_first(down, -1), along_first(up, 1), along_first(across, 2)


def place_kernel(where_ref, a_ref, b_ref, c_ref, d_ref, onehot_ref, weight_ref, keep_ref, give_ref):
    rows = (a_ref[...].astype(F32) + b_ref[...].astype(F32)) + (c_ref[...].astype(F32) + d_ref[...].astype(F32))
    placed = jnp.dot(onehot_ref[...], rows.astype(BF16), preferred_element_type=F32)
    weighted = (placed * weight_ref[:, :1]).astype(BF16)

    @pl.when(pl.program_id(1) == 0)
    def _():
        keep_ref[0] = weighted

    @pl.when(pl.program_id(1) == 1)
    def _():
        give_ref[0] = weighted


def place(where, terms, onehot, slot_weight, width):
    count = onehot.shape[0]
    cols = width // 8
    term = pl.BlockSpec((SLOTS, cols), lambda k, p, where: (0, 2 * k + (p + where[1]) % 2))
    block = pl.BlockSpec((1, count, cols), lambda k, p, where: (k, 0, 0))
    return pl.pallas_call(
        place_kernel,
        out_shape=(shape((SIDE, count, cols), BF16),) * 2,
        grid_spec=pltpu.PrefetchScalarGridSpec(
            num_scalar_prefetch=1,
            grid=(SIDE, 2),
            in_specs=[term] * 4
            + [
                pl.BlockSpec(onehot.shape, lambda k, p, where: (0, 0)),
                pl.BlockSpec(slot_weight.shape, lambda k, p, where: (0, 0)),
            ],
            out_specs=(block, block),
        ),
        compiler_params=params(),
        name="place",
    )(where, *terms, onehot, slot_weight)


def pair_kernel(where_ref, keep_ref, got_ref, own_ref, next_ref, last_ref, across_ref):
    for by, out in ((0, own_ref), (1, next_ref), (3, last_ref), (2, across_ref)):
        k = (where_ref[2] + by) % SIDE
        out[...] = (keep_ref[k].astype(F32) + got_ref[k].astype(F32)).astype(out.dtype)


def pair(where, keep, got):
    _, count, cols = keep.shape
    vmem = pl.BlockSpec(memory_space=pltpu.VMEM)
    return pl.pallas_call(
        pair_kernel,
        out_shape=(shape((count, cols), F32),) + (shape((count, cols), BF16),) * 3,
        in_specs=[pl.BlockSpec(memory_space=pltpu.SMEM), vmem, vmem],
        out_specs=(vmem,) * 4,
        compiler_params=params(),
        name="pair",
    )(where, keep, got)


def residual_kernel(where_ref, tokens_ref, own_ref, a_ref, b_ref, c_ref, mixed_ref):
    summed = (own_ref[...] + a_ref[...].astype(F32)) + (b_ref[...].astype(F32) + c_ref[...].astype(F32))
    mixed_ref[...] = (tokens_ref[...].astype(F32) + summed).astype(BF16)


def residual(where, tokens, own, others):
    count, cols = own.shape
    whole = pl.BlockSpec((count, cols), lambda i, where: (0, 0))
    return pl.pallas_call(
        residual_kernel,
        out_shape=shape((count, cols), BF16),
        grid_spec=pltpu.PrefetchScalarGridSpec(
            num_scalar_prefetch=1,
            grid=(1,),
            in_specs=[pl.BlockSpec((count, cols), lambda i, where: (0, where[0]))] + [whole] * 4,
            out_specs=whole,
        ),
        compiler_params=params(),
        name="residual",
    )(where, tokens, own, *others)


def spread(per_head, lanes):
    heads = per_head.shape[1]
    pairs = []
    first = lax.broadcasted_iota(jnp.int32, (per_head.shape[0], 2 * HEAD_DIM), 1) < HEAD_DIM
    for k in range(heads // 2):
        pairs.append(jnp.where(first, per_head[:, 2 * k : 2 * k + 1], per_head[:, 2 * k + 1 : 2 * k + 2]))
    return jnp.concatenate(pairs, axis=1)


def project_kernel(
    where_ref, mine_ref, other_ref, gain_ref, in_w_ref, write_w_ref, read_w_ref, step_w_ref, bias_ref, decay_ref,
    x_ref, write_ref, read_ref, step_ref, cum_ref, state_ref,
    in_acc, write_acc, read_acc, step_acc, square_acc,
):
    at = pl.program_id(0)

    @pl.when(at == 0)
    def _():
        for acc in (in_acc, write_acc, read_acc, step_acc, square_acc):
            acc[...] = jnp.zeros_like(acc)

    def add(block):
        values = block.astype(F32)
        square_acc[...] += jnp.sum(values * values, axis=1, keepdims=True)
        scaled = (values * gain_ref[...]).astype(BF16)
        for acc, weight in (
            (in_acc, in_w_ref), (write_acc, write_w_ref), (read_acc, read_w_ref), (step_acc, step_w_ref)
        ):
            acc[...] += jnp.dot(scaled, weight[...], preferred_element_type=F32)

    @pl.when(at < SIDE)
    def _():
        add(mine_ref[0])

    @pl.when(at >= SIDE)
    def _():
        add(other_ref[0])

    @pl.when(at == 2 * SIDE - 1)
    def _():
        count, heads = step_acc.shape
        scale = lax.rsqrt(square_acc[:, :1] / gain_ref.shape[1] / (2 * SIDE) + EPSILON)
        x = (in_acc[...] * scale).astype(BF16)
        x_ref[...] = x
        write = (write_acc[...] * scale).astype(BF16)
        write_ref[...] = write
        read_ref[...] = (read_acc[...] * scale).astype(BF16)
        raw = step_acc[...] * scale + bias_ref[...]
        step = jnp.maximum(raw, 0.0) + jnp.log1p(jnp.exp(-jnp.abs(raw)))
        step_ref[...] = step
        log_decay = -step * jnp.exp(decay_ref[...])
        lower = lax.broadcasted_iota(jnp.int32, (count, count), 0) >= lax.broadcasted_iota(jnp.int32, (count, count), 1)
        cum = jnp.dot(lower.astype(F32), log_decay, preferred_element_type=F32, precision=PRECISE)
        cum_ref[...] = cum
        last = cum[count - 1 :, :]
        to_end = jnp.exp(last - cum) * step
        weighted = (x.astype(F32) * spread(to_end, x.shape[1])).astype(BF16)
        state = lax.dot_general(write, weighted, (((0,), (0,)), ((), ())), preferred_element_type=F32)
        state_ref[:STATE, :] = state.astype(BF16)
        total = spread(last, x.shape[1])
        high = total.astype(BF16).astype(F32)
        row = lax.broadcasted_iota(jnp.int32, (16, x.shape[1]), 0)
        state_ref[STATE:, :] = jnp.where(row == 0, high, jnp.where(row == 1, total - high, 0.0)).astype(BF16)


def project(order, mine, other, gain, in_w, write_w, read_w, step_w, bias, decay_log):
    _, count, cols = mine.shape
    lanes, heads = in_w.shape[1], step_w.shape[1]
    by_rows = lambda w: pl.BlockSpec((cols, w.shape[1]), lambda i, order: (order[i], 0))
    fixed = lambda dims: pl.BlockSpec(dims, lambda i, order: (0,) * len(dims))
    outs = (
        shape((count, lanes), BF16), shape((count, STATE), BF16), shape((count, STATE), BF16),
        shape((count, heads), F32), shape((count, heads), F32), shape((STATE + 16, lanes), BF16),
    )
    return pl.pallas_call(
        project_kernel,
        out_shape=outs,
        grid_spec=pltpu.PrefetchScalarGridSpec(
            num_scalar_prefetch=1,
            grid=(2 * SIDE,),
            in_specs=[
                pl.BlockSpec((1, count, cols), lambda i, order: (jnp.minimum(i, SIDE - 1), 0, 0)),
                pl.BlockSpec((1, count, cols), lambda i, order: (jnp.maximum(i - SIDE, 0), 0, 0)),
                pl.BlockSpec((1, cols), lambda i, order: (0, order[i])),
                by_rows(in_w), by_rows(write_w), by_rows(read_w), by_rows(step_w),
                fixed((1, heads)), fixed((1, heads)),
            ],
            out_specs=tuple(fixed(o.shape) for o in outs),
            scratch_shapes=[
                pltpu.VMEM((count, lanes), F32), pltpu.VMEM((count, STATE), F32), pltpu.VMEM((count, STATE), F32),
                pltpu.VMEM((count, heads), F32), pltpu.VMEM((count, 128), F32),
            ],
        ),
        compiler_params=params(),
        name="project",
    )(
        order, mine, other, gain.reshape(1, -1), in_w, write_w, read_w, step_w,
        bias.reshape(1, -1), decay_log.reshape(1, -1),
    )


def inside_kernel(x_ref, write_ref, read_ref, step_ref, cum_ref, skip_ref, out_ref):
    count, heads = step_ref.shape
    span = count // 2
    scores = lax.dot_general(read_ref[...], write_ref[...], (((1,), (1,)), ((), ())), preferred_element_type=F32)
    cum = cum_ref[...]
    cum_t, step_t = cum.T, step_ref[...].T
    causal = lax.broadcasted_iota(jnp.int32, (span, span), 0) >= lax.broadcasted_iota(jnp.int32, (span, span), 1)
    low, high = slice(0, span), slice(span, count)

    def mixing(h, rows, columns):
        gaps = cum[rows, h : h + 1] - cum_t[h : h + 1, columns]
        if rows == columns:
            gaps = jnp.where(causal, gaps, -jnp.inf)
        return (scores[rows, columns] * jnp.exp(gaps) * step_t[h : h + 1, columns]).astype(BF16)

    for h in range(heads):
        lanes = slice(h * HEAD_DIM, (h + 1) * HEAD_DIM)
        x = x_ref[:, lanes]
        skipped = skip_ref[0, h] * x.astype(F32)
        top = jnp.dot(mixing(h, low, low), x[low], preferred_element_type=F32)
        below = jnp.concatenate([mixing(h, high, low), mixing(h, high, high)], axis=1)
        bottom = jnp.dot(below, x, preferred_element_type=F32)
        out_ref[:, lanes] = jnp.concatenate([top, bottom], axis=0) + skipped


def inside(x, write, read, step, cum, skip_gain):
    vmem = pl.BlockSpec(memory_space=pltpu.VMEM)
    return pl.pallas_call(
        inside_kernel,
        out_shape=shape(x.shape, F32),
        in_specs=[vmem] * 5 + [pl.BlockSpec(memory_space=pltpu.SMEM)],
        out_specs=vmem,
        compiler_params=params(),
        cost_estimate=pl.CostEstimate(flops=2 * 10**9, bytes_accessed=2 * 10**6, transcendentals=10**6),
        name="inside",
    )(x, write, read, step, cum, skip_gain.reshape(1, -1))


def log_of(ref):
    return ref[STATE : STATE + 1, :].astype(F32) + ref[STATE + 1 : STATE + 2, :].astype(F32)


def weights_before(here, places, logs):
    terms = []
    for s in places:
        between = sum(jnp.where((s < u) & (u < here), log, 0.0) for u, log in zip(places, logs))
        terms.append(jnp.where(s < here, jnp.exp(between), 0.0))
    return terms


def ring_kernel(where_ref, own_ref, last_ref, next_ref, across_ref, prior_ref, total_ref):
    here = where_ref[3]
    refs = (own_ref, last_ref, next_ref, across_ref)
    places = [here, (here + 3) % SIDE, (here + 1) % SIDE, (here + 2) % SIDE]
    logs = [log_of(ref) for ref in refs]
    before = weights_before(here, places, logs)
    until_end = [jnp.exp(sum(jnp.where(s < u, log, 0.0) for u, log in zip(places, logs))) for s in places]
    states = [ref[:STATE, :].astype(F32) for ref in refs]
    prior_ref[:STATE, :] = sum(w * s for w, s in zip(before, states))
    gone = sum(jnp.where(s < here, log, 0.0) for s, log in zip(places, logs))
    prior_ref[STATE:, :] = jnp.broadcast_to(jnp.exp(gone), (8, gone.shape[1]))
    total_ref[:STATE, :] = sum(w * s for w, s in zip(until_end, states)).astype(BF16)
    whole = sum(logs)
    top = whole.astype(BF16).astype(F32)
    row = lax.broadcasted_iota(jnp.int32, (16, whole.shape[1]), 0)
    total_ref[STATE:, :] = jnp.where(row == 0, top, jnp.where(row == 1, whole - top, 0.0)).astype(BF16)


def ring(where, parts):
    vmem = pl.BlockSpec(memory_space=pltpu.VMEM)
    lanes = parts[0].shape[1]
    return pl.pallas_call(
        ring_kernel,
        out_shape=(shape((STATE + 8, lanes), F32), shape((STATE + 16, lanes), BF16)),
        in_specs=[pl.BlockSpec(memory_space=pltpu.SMEM)] + [vmem] * 4,
        out_specs=(vmem, vmem),
        compiler_params=params(),
        name="ring",
    )(where, *parts)


def finish_kernel(where_ref, prior_ref, last_ref, next_ref, across_ref, read_ref, cum_ref, inside_ref, out_ref):
    here = where_ref[4]
    refs = (last_ref, next_ref, across_ref)
    places = [(here + 3) % SIDE, (here + 1) % SIDE, (here + 2) % SIDE]
    logs = [log_of(ref) for ref in refs]
    before = weights_before(here, places, logs)
    earlier = sum(w * ref[:STATE, :].astype(F32) for w, ref in zip(before, refs))
    carried = (prior_ref[:STATE, :] + prior_ref[STATE : STATE + 1, :] * earlier).astype(BF16)
    from_prior = jnp.dot(read_ref[...], carried, preferred_element_type=F32)
    decayed = spread(jnp.exp(cum_ref[...]), carried.shape[1])
    out_ref[...] = (inside_ref[...] + decayed * from_prior).astype(BF16)


def finish(where, prior, parts, read, cum, within):
    vmem = pl.BlockSpec(memory_space=pltpu.VMEM)
    return pl.pallas_call(
        finish_kernel,
        out_shape=shape(within.shape, BF16),
        in_specs=[pl.BlockSpec(memory_space=pltpu.SMEM)] + [vmem] * 7,
        out_specs=vmem,
        compiler_params=params(),
        name="finish",
    )(where, prior, *parts, read, cum, within)


def body(
    tokens,
    routes,
    route_weight,
    moe_gain,
    gate_weight,
    up_weight,
    down_weight,
    ssd_gain,
    input_weight,
    write_weight,
    read_weight,
    step_weight,
    step_bias,
    decay_log,
    skip_gain,
):
    width = tokens.shape[1]
    expert, frame = lax.axis_index("expert"), lax.axis_index("frame")
    y, core, z, x = expert // 2, expert % 2, frame // SIDE, frame % SIDE
    where = jnp.stack([expert, core, y, x, z]).astype(jnp.int32)
    rows, onehot, slot_weight = pick(where, tokens, routes, route_weight, moe_gain)
    terms = experts(rows, gate_weight[0], up_weight[0], down_weight[0])
    keep, give = place(where, terms, onehot, slot_weight, width)
    own, to_next, to_last, to_across = pair(where, keep, to_sibling(give))
    others = (along_y(to_next, 1), along_y(to_last, -1), along_y(to_across, 2))
    mixed = residual(where, tokens, own, others)
    mine = jnp.stack([mixed, along_y(mixed, 1), along_y(mixed, -1), along_y(mixed, 2)])
    other = to_sibling(mine)
    around = jnp.stack([y, (y + 3) % SIDE, (y + 1) % SIDE, (y + 2) % SIDE])
    order = jnp.concatenate([2 * around + core, 2 * around + 1 - core]).astype(jnp.int32)
    inputs, write, read, step, cum, state = project(
        order, mine, other, ssd_gain, input_weight, write_weight, read_weight, step_weight, step_bias, decay_log
    )
    parts = (state, along_x(state, 1), along_x(state, -1), along_x(state, 2))
    prior, total = ring(where, parts)
    earlier = (along_z(total, 1), along_z(total, -1), along_z(total, 2))
    within = inside(inputs, write, read, step, cum, skip_gain)
    ssd_out = finish(where, prior, earlier, read, cum, within)
    return (mixed, ssd_out)


def solution(mesh):
    placed = (
        P("frame", None),
        P("frame", None),
        P("frame", None),
        P(),
        P("expert", "frame", None),
        P("expert", "frame", None),
        P("expert", "frame", None),
        P(),
        P(None, "expert"),
        P(None, "expert"),
        P(None, "expert"),
        P(None, "expert"),
        P("expert"),
        P("expert"),
        P("expert"),
    )
    return jax.shard_map(
        body,
        mesh=mesh,
        in_specs=placed,
        out_specs=(P("frame", "expert"), P("frame", "expert")),
        check_vma=False,
    )
```

time: 424 us -> 308 us (0.73)
  waiting for transfers between devices: 270 us -> 156 us
  starting transfers between devices: 0.34 us -> 45.9 us
  Pallas kernels: 0 us -> 24.3 us
  local copies, waits for them, and re-layouts: 36.7 us -> 17.5 us
  blocking collectives: 17.2 us -> 0 us
  matrix products: 67.7 us -> 52 us
  between operations: 14.1 us -> 1.5 us
  other arithmetic: 16.3 us -> 5.81 us
    ppermute x0 -> x28, waiting for transfers between devices: none -> 156 us  [send(): return lax.ppermute(array, AXES, routes_of(rule))]
    all_gather x2 -> x0, waiting for transfers between devices: 113 us -> none  [the longest x1 93.5 us: body(): piece = lax.all_gather(picked, 'frame', axis=0, tiled=True)]
    reduce_scatter x1 -> x0, waiting for transfers between devices: 93.5 us -> none  [body(): lax.psum_scatter(jnp.dot(hidden, down_w, preferred_element_type=jnp.float...]
    psum x1 -> x0, waiting for transfers between devices: 63 us -> none  [body(): lax.psum(weighted.astype(jnp.bfloat16), 'expert').astype(jnp.float32)]
    ppermute x0 -> x28, starting transfers between devices: none -> 45.9 us  [send(): return lax.ppermute(array, AXES, routes_of(rule))]
    pallas_call x0 -> x8, Pallas kernels: none -> 24.3 us  [the longest x1 11 us: project(): pl.pallas_call(project_kernel, out_shape=outs, grid_spec=pltpu.PrefetchSc...]
    dynamic_slice x33 -> x0, local copies, waits for them, and re-layouts: 21.8 us -> none  [the longest x32 20.1 us: turn(): part[k].astype(own.dtype)]
    all_gather x1 -> x0, blocking collectives: 17.2 us -> none  [carried_in(): lax.all_gather(part.astype(kind), axis)]
  transfers between devices with their start and end apart: 4 -> 28, of which waited for: 4 -> 22; matrix products, arithmetic and copies ran while one was open for 4% -> 13% of each run, Pallas kernels for 0% -> 1%
where the time goes in v1:
time: 308 us; the launch traced here: 303 us
  waiting for transfers between devices  156 us (51%)
  matrix products  52 us (17%)
  starting transfers between devices  45.9 us (15%)
  Pallas kernels  24.3 us (8%)
  local copies, waits for them, and re-layouts  17.5 us (6%)
  other arithmetic  5.81 us (2%)
    ppermute x28, waiting for transfers between devices, send(): return lax.ppermute(array, AXES, routes_of(rule))  156 us
    ppermute x28, starting transfers between devices, send(): return lax.ppermute(array, AXES, routes_of(rule))  45.9 us
    dot_general x4, matrix products, expert_out(): jnp.dot(expert_hidden(rows, gate_w, up_w), down_w, preferred_element_type...  38.3 us
    dot_general x4, matrix products, expert_hidden(): upper = jnp.einsum('rd,fd->rf', rows, up_w, preferred_element_type=F32)  13.8 us
    unnamed x51, local copies, waits for them, and re-layouts  12 us
    pallas_call x1, Pallas kernels, project(): pl.pallas_call(project_kernel, out_shape=outs, grid_spec=pltpu.PrefetchSc...  11 us
  transfers between devices with their start and end apart: 28, of which 22 were waited for; matrix products, arithmetic and copies ran while one was open for 13% of the time, Pallas kernels for 1%

profile of v1, /device:TPU:1, one launch (start us, length us, event | category | flops | bytes accessed | tf_op | source)
XLA Modules:
  0.0 303.5 jit_solution(3656583380514450263)
XLA Ops:
  12.3 8.3 %collective-permute-done = bf16[96,4096]{1,0:T(8,128)(2,1)S(1)} collective-permute-done((bf16[96,4096]{1,0:T(8,128)(2,1)S(1)}, bf16[96,4096]{1,0:T(8,128)(2,1)S(1)}, u32[]{:S(2)}, u32[]{:S(2)}) %collective-permute-start) | collective-permute-done | bytes 786464 | tf_op jit(solution)/shard_map/ppermute | solution.py:35
  20.6 7.7 %collective-permute-done.1 = bf16[96,4096]{1,0:T(8,128)(2,1)S(1)} collective-permute-done((bf16[96,4096]{1,0:T(8,128)(2,1)S(1)}, bf16[96,4096]{1,0:T(8,128)(2,1)S(1)}, u32[]{:S(2)}, u32[]{:S(2)}) %collective-permute-start.1) | collective-permute-done | bytes 786464 | tf_op jit(solution)/shard_map/ppermute | solution.py:35
  32.9 34.9 %collective-permute-done.4 = bf16[384,4096]{1,0:T(8,128)(2,1)S(1)} collective-permute-done((bf16[384,4096]{1,0:T(8,128)(2,1)S(1)}, bf16[384,4096]{1,0:T(8,128)(2,1)S(1)}, u32[]{:S(2)}, u32[]{:S(2)}) %collective-permute-start.4) | collective-permute-done | bytes 3145760 | tf_op jit(solution)/shard_map/ppermute | solution.py:35
  75.2 9.9 %convolution_convert_fusion.2 = bf16[384,4096]{1,0:T(8,128)(2,1)} fusion(bf16[1,448,4096]{2,1,0:T(8,128)(2,1)} %param.21, f32[384,448]{0,1:T(8,128)} %fusion.8, bf16[384,4096]{1,0:T(8,128)(2,1)} %copy-done.13, bf16[1,448,4096]{2,1,0:T(8,128)(2,1)} %param.19), kind=kOutput, calls=%fused_computation.3 | convolution fusion | flops 2821177344 | bytes 14319616 | tf_op jit(solution)/shard_map/dot_general | solution.py:107
  85.0 3.8 %collective-permute-done.5 = bf16[192,4096]{1,0:T(8,128)(2,1)S(1)} collective-permute-done((bf16[192,4096]{1,0:T(8,128)(2,1)S(1)}, bf16[192,4096]{1,0:T(8,128)(2,1)S(1)}, u32[]{:S(2)}, u32[]{:S(2)}) %collective-permute-start.5) | collective-permute-done | bytes 1572896 | tf_op jit(solution)/shard_map/ppermute | solution.py:35
  96.2 8.2 %convolution_convert_fusion.1 = bf16[384,4096]{1,0:T(8,128)(2,1)S(1)} fusion(bf16[1,448,4096]{2,1,0:T(8,128)(2,1)} %param.21, f32[384,448]{0,1:T(8,128)} %fusion.6, bf16[384,4096]{1,0:T(8,128)(2,1)} %copy-done.14, bf16[1,448,4096]{2,1,0:T(8,128)(2,1)} %param.19), kind=kOutput, calls=%fused_computation.2 | convolution fusion | flops 2821177344 | bytes 14319616 | tf_op jit(solution)/shard_map/dot_general | solution.py:107
  107.4 5.0 %fusion.4 = f32[384,448]{0,1:T(8,128)} fusion(bf16[384,4096]{1,0:T(8,128)(2,1)S(1)} %copy-done.12, bf16[1,448,4096]{2,1,0:T(8,128)(2,1)} %param.20), kind=kOutput, calls=%fused_computation.9 | convolution fusion | flops 1409286144 | bytes 7503872 | tf_op jit(solution)/shard_map/rd,fd->rf/dot_general | solution.py:102
  112.3 3.4 %collective-permute-start.9 = (bf16[192,4096]{1,0:T(8,128)(2,1)}, bf16[192,4096]{1,0:T(8,128)(2,1)}, u32[]{:S(2)}, u32[]{:S(2)}) collective-permute-start(bf16[192,4096]{1,0:T(8,128)(2,1)} %get-tuple-element.43), channel_id=1, source_target_pairs={{0,12},{1,13},{2,14},{3,15},{4,0},{5,1},{6,2},{7,3},{8,4},{9,5},{1... | collective-permute-start | bytes 4718600 | tf_op jit(solution)/shard_map/ppermute | solution.py:35
  115.7 9.9 %convolution_convert_fusion = bf16[384,4096]{1,0:T(8,128)(2,1)} fusion(bf16[1,448,4096]{2,1,0:T(8,128)(2,1)} %param.21, f32[384,448]{0,1:T(8,128)} %fusion.4, bf16[384,4096]{1,0:T(8,128)(2,1)} %copy-done.11, bf16[1,448,4096]{2,1,0:T(8,128)(2,1)} %param.19), kind=kOutput, calls=%fused_computation.1 | convolution fusion | flops 2821177344 | bytes 14319616 | tf_op jit(solution)/shard_map/dot_general | solution.py:107
  141.9 25.9 %collective-permute-done.8 = bf16[384,4096]{1,0:T(8,128)(2,1)S(1)} collective-permute-done((bf16[384,4096]{1,0:T(8,128)(2,1)S(1)}, bf16[384,4096]{1,0:T(8,128)(2,1)S(1)}, u32[]{:S(2)}, u32[]{:S(2)}) %collective-permute-start.8) | collective-permute-done | bytes 3145760 | tf_op jit(solution)/shard_map/ppermute | solution.py:35
  169.5 3.7 %collective-permute-done.10 = bf16[384,4096]{1,0:T(8,128)(2,1)} collective-permute-done((bf16[384,4096]{1,0:T(8,128)(2,1)S(1)}, bf16[384,4096]{1,0:T(8,128)(2,1)}, u32[]{:S(2)}, u32[]{:S(2)}) %collective-permute-start.10) | collective-permute-done | bytes 3145760 | tf_op jit(solution)/shard_map/ppermute | solution.py:35
  173.1 10.3 %add_convert_fusion = bf16[384,4096]{1,0:T(8,128)(2,1)S(1)} fusion(bf16[384,4096]{1,0:T(8,128)(2,1)} %collective-permute-done.10, bf16[384,4096]{1,0:T(8,128)(2,1)} %copy-done.21, bf16[1,448,4096]{2,1,0:T(8,128)(2,1)} %param.21, f32[384,448]{0,1:T(8,128)} %fusion.10, bf16[384,4096]{1,0:T(8,128)(2,1)} %copy-done.15, bf16[1,448,4096]{2,1,0:T(8,128)(2,1)} %param.19), kind=kOutput, calls=%fused_computation | convolution fusion | flops 2830614528 | bytes 20611072 | tf_op jit(solution)/shard_map/dot_general | solution.py:107
  187.4 15.9 %collective-permute-done.11.b_ref = bf16[96,4096]{1,0:T(8,128)(2,1)S(1)} collective-permute-done((bf16[96,4096]{1,0:T(8,128)(2,1)S(1)}, bf16[96,4096]{1,0:T(8,128)(2,1)S(1)}, u32[]{:S(2)}, u32[]{:S(2)}) %collective-permute-start.11) | collective-permute-done | bytes 786464 | tf_op jit(solution)/shard_map/ppermute | solution.py:35
  203.3 3.4 %collective-permute-done.12.c_ref = bf16[96,4096]{1,0:T(8,128)(2,1)S(1)} collective-permute-done((bf16[96,4096]{1,0:T(8,128)(2,1)S(1)}, bf16[96,4096]{1,0:T(8,128)(2,1)S(1)}, u32[]{:S(2)}, u32[]{:S(2)}) %collective-permute-start.12) | collective-permute-done | bytes 786464 | tf_op jit(solution)/shard_map/ppermute | solution.py:35
  206.7 3.6 %place.1 = (bf16[4,256,512]{2,1,0:T(8,128)(2,1)S(1)}, bf16[4,256,512]{2,1,0:T(8,128)(2,1)S(1)}) custom-call(s32[5]{0:T(128)S(1)} %stack.51.where_ref, bf16[96,4096]{1,0:T(8,128)(2,1)S(1)} %get-tuple-element.41.a_ref, bf16[96,4096]{1,0:T(8,128)(2,1)S(1)} %collective-permute-done.11.b_ref, bf16[96,4096]{1,0:T(8,128)(2,1)S(1)} %collective-permute-done.12.c_ref, ...), custom_call_target="tpu_custom_call" | custom-call | tf_op jit(solution)/shard_map/place/pallas_call | solution.py:156
  210.3 6.4 %collective-permute-start.14 = (bf16[4,256,512]{2,1,0:T(8,128)(2,1)S(1)}, bf16[4,256,512]{2,1,0:T(8,128)(2,1)S(1)}, u32[]{:S(2)}, u32[]{:S(2)}) collective-permute-start(bf16[4,256,512]{2,1,0:T(8,128)(2,1)S(1)} %get-tuple-element.23), channel_id=1, source_target_pairs={{0,16},{1,17},{2,18},{3,19},{4,20},{5,21},{6,22},{7,23},{8,24},{9,... | collective-permute-start | bytes 3145736 | tf_op jit(solution)/shard_map/ppermute | solution.py:35
  224.2 4.5 %collective-permute-done.15.a_ref = bf16[256,512]{1,0:T(8,128)(2,1)S(1)} collective-permute-done((bf16[256,512]{1,0:T(8,128)(2,1)S(1)}, bf16[256,512]{1,0:T(8,128)(2,1)S(1)}, u32[]{:S(2)}, u32[]{:S(2)}) %collective-permute-start.15) | collective-permute-done | bytes 262176 | tf_op jit(solution)/shard_map/ppermute | solution.py:35
  228.7 6.7 %collective-permute-done.17.c_ref = bf16[256,512]{1,0:T(8,128)(2,1)S(1)} collective-permute-done((bf16[256,512]{1,0:T(8,128)(2,1)S(1)}, bf16[256,512]{1,0:T(8,128)(2,1)S(1)}, u32[]{:S(2)}, u32[]{:S(2)}) %collective-permute-start.17) | collective-permute-done | bytes 262176 | tf_op jit(solution)/shard_map/ppermute | solution.py:35
  239.5 6.2 %collective-permute-done.18 = bf16[256,512]{1,0:T(8,128)(2,1)S(1)} collective-permute-done((bf16[256,512]{1,0:T(8,128)(2,1)}, bf16[256,512]{1,0:T(8,128)(2,1)S(1)}, u32[]{:S(2)}, u32[]{:S(2)}) %collective-permute-start.18) | collective-permute-done | bytes 262176 | tf_op jit(solution)/shard_map/ppermute | solution.py:35
  245.7 3.9 %collective-permute-done.20 = bf16[256,512]{1,0:T(8,128)(2,1)S(1)} collective-permute-done((bf16[256,512]{1,0:T(8,128)(2,1)}, bf16[256,512]{1,0:T(8,128)(2,1)S(1)}, u32[]{:S(2)}, u32[]{:S(2)}) %collective-permute-start.20) | collective-permute-done | bytes 262176 | tf_op jit(solution)/shard_map/ppermute | solution.py:35
  256.2 11.0 %project.1 = (bf16[256,1024]{1,0:T(8,128)(2,1)S(1)}, bf16[256,128]{1,0:T(8,128)(2,1)S(1)}, bf16[256,128]{1,0:T(8,128)(2,1)S(1)}, f32[256,16]{1,0:T(8,128)S(1)}, ...) custom-call(s32[8]{0:T(128)S(1)} %pad_add_fusion.where_ref, bf16[4,256,512]{2,1,0:T(8,128)(2,1)S(1)} %pad_maximum_fusion.2.mine_ref, ...), custom_call_target="tpu_custom_call" | custom-call | tf_op jit(solution)/shard_map/project/pallas_call | solution.py:289
  270.0 13.1 %collective-permute-done.22.last_ref = bf16[144,1024]{1,0:T(8,128)(2,1)S(1)} collective-permute-done((bf16[144,1024]{1,0:T(8,128)(2,1)S(1)}, bf16[144,1024]{1,0:T(8,128)(2,1)S(1)}, u32[]{:S(2)}, u32[]{:S(2)}) %collective-permute-start.22) | collective-permute-done | bytes 294944 | tf_op jit(solution)/shard_map/ppermute | solution.py:35
  284.1 3.6 %collective-permute-start.26 = (bf16[144,1024]{1,0:T(8,128)(2,1)S(1)}, bf16[144,1024]{1,0:T(8,128)(2,1)S(1)}, u32[]{:S(2)}, u32[]{:S(2)}) collective-permute-start(bf16[144,1024]{1,0:T(8,128)(2,1)S(1)} %get-tuple-element.30), channel_id=1, source_target_pairs={{0,12},{1,13},{2,14},{3,15},{4,0},{5,1},{6,2},{7,3},{8,4},{9,5},{1... | collective-permute-start | bytes 884744 | tf_op jit(solution)/shard_map/ppermute | solution.py:35
  293.7 5.2 %collective-permute-done.26.next_ref = bf16[144,1024]{1,0:T(8,128)(2,1)S(1)} collective-permute-done((bf16[144,1024]{1,0:T(8,128)(2,1)S(1)}, bf16[144,1024]{1,0:T(8,128)(2,1)S(1)}, u32[]{:S(2)}, u32[]{:S(2)}) %collective-permute-start.26) | collective-permute-done | bytes 294944 | tf_op jit(solution)/shard_map/ppermute | solution.py:35
  (116 shorter events, 87.7 us)
Async XLA Ops:
  6.3 14.3 %collective-permute-start = (bf16[96,4096]{1,0:T(8,128)(2,1)S(1)}, bf16[96,4096]{1,0:T(8,128)(2,1)S(1)}, u32[]{:S(2)}, u32[]{:S(2)}) collective-permute-start(bf16[96,4096]{1,0:T(8,128)(2,1)S(1)} %get-tuple-element.19), channel_id=1, source_target_pairs={{0,1},{1,2},{2,3},{3,0},{4,5},{5,6},{6,7},{7,4},{8,9},{9,10},{10,1... | collective-permute-start | bytes 2359304 | tf_op jit(solution)/shard_map/ppermute | solution.py:35
  8.8 19.6 %collective-permute-start.1 = (bf16[96,4096]{1,0:T(8,128)(2,1)S(1)}, bf16[96,4096]{1,0:T(8,128)(2,1)S(1)}, u32[]{:S(2)}, u32[]{:S(2)}) collective-permute-start(bf16[96,4096]{1,0:T(8,128)(2,1)S(1)} %get-tuple-element.19), channel_id=1, source_target_pairs={{0,3},{1,0},{2,1},{3,2},{4,7},{5,4},{6,5},{7,6},{8,11},{9,8},{10,9... | collective-permute-start | bytes 2359304 | tf_op jit(solution)/shard_map/ppermute | solution.py:35
  11.0 19.1 %collective-permute-start.2 = (bf16[96,4096]{1,0:T(8,128)(2,1)S(1)}, bf16[96,4096]{1,0:T(8,128)(2,1)S(1)}, u32[]{:S(2)}, u32[]{:S(2)}) collective-permute-start(bf16[96,4096]{1,0:T(8,128)(2,1)S(1)} %get-tuple-element.19), channel_id=1, source_target_pairs={{0,2},{1,3},{2,0},{3,1},{4,6},{5,7},{6,4},{7,5},{8,10},{9,11},{10,... | collective-permute-start | bytes 2359304 | tf_op jit(solution)/shard_map/ppermute | solution.py:35
  30.1 37.7 %collective-permute-start.4 = (bf16[384,4096]{1,0:T(8,128)(2,1)S(1)}, bf16[384,4096]{1,0:T(8,128)(2,1)S(1)}, u32[]{:S(2)}, u32[]{:S(2)}) collective-permute-start(bf16[384,4096]{1,0:T(8,128)(2,1)S(1)} %constant_dynamic-update-slice_fusion), channel_id=1, source_target_pairs={{0,4},{1,5},{2,6},{3,7},{4,8},{5,9},{6,10},{7,11},{8,12},{9,13},{1... | collective-permute-start | bytes 9437192 | tf_op jit(solution)/shard_map/ppermute | solution.py:35
  31.3 36.8 %collective-permute-start.3 = (bf16[384,4096]{1,0:T(8,128)(2,1)S(1)}, bf16[384,4096]{1,0:T(8,128)(2,1)S(1)}, u32[]{:S(2)}, u32[]{:S(2)}) collective-permute-start(bf16[384,4096]{1,0:T(8,128)(2,1)S(1)} %constant_dynamic-update-slice_fusion), channel_id=1, source_target_pairs={{0,12},{1,13},{2,14},{3,15},{4,0},{5,1},{6,2},{7,3},{8,4},{9,5},{1... | collective-permute-start | bytes 9437192 | tf_op jit(solution)/shard_map/ppermute | solution.py:35
  68.0 20.8 %collective-permute-start.5 = (bf16[192,4096]{1,0:T(8,128)(2,1)S(1)}, bf16[192,4096]{1,0:T(8,128)(2,1)S(1)}, u32[]{:S(2)}, u32[]{:S(2)}) collective-permute-start(bf16[192,4096]{1,0:T(8,128)(2,1)S(1)} %slice.49), channel_id=1, source_target_pairs={{0,4},{1,5},{2,6},{3,7},{4,8},{5,9},{6,10},{7,11},{8,12},{9,13},{1... | collective-permute-start | bytes 4718600 | tf_op jit(solution)/shard_map/ppermute | solution.py:35
  70.0 20.0 %collective-permute-start.6 = (bf16[192,4096]{1,0:T(8,128)(2,1)}, bf16[192,4096]{1,0:T(8,128)(2,1)}, u32[]{:S(2)}, u32[]{:S(2)}) collective-permute-start(bf16[192,4096]{1,0:T(8,128)(2,1)} %slice.50), channel_id=1, source_target_pairs={{0,12},{1,13},{2,14},{3,15},{4,0},{5,1},{6,2},{7,3},{8,4},{9,5},{1... | collective-permute-start | bytes 4718600 | tf_op jit(solution)/shard_map/ppermute | solution.py:35
  106.2 21.6 %collective-permute-start.7 = (bf16[192,4096]{1,0:T(8,128)(2,1)}, bf16[192,4096]{1,0:T(8,128)(2,1)}, u32[]{:S(2)}, u32[]{:S(2)}) collective-permute-start(bf16[192,4096]{1,0:T(8,128)(2,1)} %get-tuple-element.42), channel_id=1, source_target_pairs={{0,4},{1,5},{2,6},{3,7},{4,8},{5,9},{6,10},{7,11},{8,12},{9,13},{1... | collective-permute-start | bytes 4718600 | tf_op jit(solution)/shard_map/ppermute | solution.py:35
  112.3 21.1 %collective-permute-start.9 = (bf16[192,4096]{1,0:T(8,128)(2,1)}, bf16[192,4096]{1,0:T(8,128)(2,1)}, u32[]{:S(2)}, u32[]{:S(2)}) collective-permute-start(bf16[192,4096]{1,0:T(8,128)(2,1)} %get-tuple-element.43), channel_id=1, source_target_pairs={{0,12},{1,13},{2,14},{3,15},{4,0},{5,1},{6,2},{7,3},{8,4},{9,5},{1... | collective-permute-start | bytes 4718600 | tf_op jit(solution)/shard_map/ppermute | solution.py:35
  130.1 37.7 %collective-permute-start.8 = (bf16[384,4096]{1,0:T(8,128)(2,1)S(1)}, bf16[384,4096]{1,0:T(8,128)(2,1)S(1)}, u32[]{:S(2)}, u32[]{:S(2)}) collective-permute-start(bf16[384,4096]{1,0:T(8,128)(2,1)S(1)} %pad_maximum_fusion), channel_id=1, source_target_pairs={{0,4},{1,5},{2,6},{3,7},{4,8},{5,9},{6,10},{7,11},{8,12},{9,13},{1... | collective-permute-start | bytes 9437192 | tf_op jit(solution)/shard_map/ppermute | solution.py:35
  135.7 37.4 %collective-permute-start.10 = (bf16[384,4096]{1,0:T(8,128)(2,1)S(1)}, bf16[384,4096]{1,0:T(8,128)(2,1)}, u32[]{:S(2)}, u32[]{:S(2)}) collective-permute-start(bf16[384,4096]{1,0:T(8,128)(2,1)S(1)} %pad_maximum_fusion.1), channel_id=1, source_target_pairs={{0,12},{1,13},{2,14},{3,15},{4,0},{5,1},{6,2},{7,3},{8,4},{9,5},{1... | collective-permute-start | bytes 9437192 | tf_op jit(solution)/shard_map/ppermute | solution.py:35
  183.7 19.6 %collective-permute-start.11 = (bf16[96,4096]{1,0:T(8,128)(2,1)S(1)}, bf16[96,4096]{1,0:T(8,128)(2,1)S(1)}, u32[]{:S(2)}, u32[]{:S(2)}) collective-permute-start(bf16[96,4096]{1,0:T(8,128)(2,1)S(1)} %get-tuple-element.40), channel_id=1, source_target_pairs={{0,3},{1,0},{2,1},{3,2},{4,7},{5,4},{6,5},{7,6},{8,11},{9,8},{10,9... | collective-permute-start | bytes 2359304 | tf_op jit(solution)/shard_map/ppermute | solution.py:35
  186.0 20.8 %collective-permute-start.12 = (bf16[96,4096]{1,0:T(8,128)(2,1)S(1)}, bf16[96,4096]{1,0:T(8,128)(2,1)S(1)}, u32[]{:S(2)}, u32[]{:S(2)}) collective-permute-start(bf16[96,4096]{1,0:T(8,128)(2,1)S(1)} %get-tuple-element.39), channel_id=1, source_target_pairs={{0,1},{1,2},{2,3},{3,0},{4,5},{5,6},{6,7},{7,4},{8,9},{9,10},{10,1... | collective-permute-start | bytes 2359304 | tf_op jit(solution)/shard_map/ppermute | solution.py:35
  186.0 20.8 %collective-permute-start.13 = (bf16[96,4096]{1,0:T(8,128)(2,1)S(1)}, bf16[96,4096]{1,0:T(8,128)(2,1)S(1)}, u32[]{:S(2)}, u32[]{:S(2)}) collective-permute-start(bf16[96,4096]{1,0:T(8,128)(2,1)S(1)} %get-tuple-element.38), channel_id=1, source_target_pairs={{0,2},{1,3},{2,0},{3,1},{4,6},{5,7},{6,4},{7,5},{8,10},{9,11},{10,... | collective-permute-start | bytes 2359304 | tf_op jit(solution)/shard_map/ppermute | solution.py:35
  219.7 8.9 %collective-permute-start.15 = (bf16[256,512]{1,0:T(8,128)(2,1)S(1)}, bf16[256,512]{1,0:T(8,128)(2,1)S(1)}, u32[]{:S(2)}, u32[]{:S(2)}) collective-permute-start(bf16[256,512]{1,0:T(8,128)(2,1)S(1)} %get-tuple-element.25), channel_id=1, source_target_pairs={{0,32},{1,33},{2,34},{3,35},{4,36},{5,37},{6,38},{7,39},{8,40},{9,... | collective-permute-start | bytes 786440 | tf_op jit(solution)/shard_map/ppermute | solution.py:35
  222.6 12.8 %collective-permute-start.17 = (bf16[256,512]{1,0:T(8,128)(2,1)S(1)}, bf16[256,512]{1,0:T(8,128)(2,1)S(1)}, u32[]{:S(2)}, u32[]{:S(2)}) collective-permute-start(bf16[256,512]{1,0:T(8,128)(2,1)S(1)} %get-tuple-element.27), channel_id=1, source_target_pairs={{0,64},{1,65},{2,66},{3,67},{4,68},{5,69},{6,70},{7,71},{8,72},{9,... | collective-permute-start | bytes 786440 | tf_op jit(solution)/shard_map/ppermute | solution.py:35
  236.8 8.9 %collective-permute-start.18 = (bf16[256,512]{1,0:T(8,128)(2,1)}, bf16[256,512]{1,0:T(8,128)(2,1)S(1)}, u32[]{:S(2)}, u32[]{:S(2)}) collective-permute-start(bf16[256,512]{1,0:T(8,128)(2,1)} %residual.1), channel_id=1, source_target_pairs={{0,32},{1,33},{2,34},{3,35},{4,36},{5,37},{6,38},{7,39},{8,40},{9,... | collective-permute-start | bytes 786440 | tf_op jit(solution)/shard_map/ppermute | solution.py:35
  239.5 10.1 %collective-permute-start.20 = (bf16[256,512]{1,0:T(8,128)(2,1)}, bf16[256,512]{1,0:T(8,128)(2,1)S(1)}, u32[]{:S(2)}, u32[]{:S(2)}) collective-permute-start(bf16[256,512]{1,0:T(8,128)(2,1)} %residual.1), channel_id=1, source_target_pairs={{0,64},{1,65},{2,66},{3,67},{4,68},{5,69},{6,70},{7,71},{8,72},{9,... | collective-permute-start | bytes 786440 | tf_op jit(solution)/shard_map/ppermute | solution.py:35
  267.2 15.8 %collective-permute-start.22 = (bf16[144,1024]{1,0:T(8,128)(2,1)S(1)}, bf16[144,1024]{1,0:T(8,128)(2,1)S(1)}, u32[]{:S(2)}, u32[]{:S(2)}) collective-permute-start(bf16[144,1024]{1,0:T(8,128)(2,1)S(1)} %get-tuple-element.28.own_ref), channel_id=1, source_target_pairs={{0,1},{1,2},{2,3},{3,0},{4,5},{5,6},{6,7},{7,4},{8,9},{9,10},{10,1... | collective-permute-start | bytes 884744 | tf_op jit(solution)/shard_map/ppermute | solution.py:35
  267.3 15.7 %collective-permute-start.23 = (bf16[144,1024]{1,0:T(8,128)(2,1)S(1)}, bf16[144,1024]{1,0:T(8,128)(2,1)S(1)}, u32[]{:S(2)}, u32[]{:S(2)}) collective-permute-start(bf16[144,1024]{1,0:T(8,128)(2,1)S(1)} %get-tuple-element.28.own_ref), channel_id=1, source_target_pairs={{0,3},{1,0},{2,1},{3,2},{4,7},{5,4},{6,5},{7,6},{8,11},{9,8},{10,9... | collective-permute-start | bytes 884744 | tf_op jit(solution)/shard_map/ppermute | solution.py:35
  270.0 13.1 %collective-permute-start.24 = (bf16[144,1024]{1,0:T(8,128)(2,1)S(1)}, bf16[144,1024]{1,0:T(8,128)(2,1)S(1)}, u32[]{:S(2)}, u32[]{:S(2)}) collective-permute-start(bf16[144,1024]{1,0:T(8,128)(2,1)S(1)} %get-tuple-element.28.own_ref), channel_id=1, source_target_pairs={{0,2},{1,3},{2,0},{3,1},{4,6},{5,7},{6,4},{7,5},{8,10},{9,11},{10,... | collective-permute-start | bytes 884744 | tf_op jit(solution)/shard_map/ppermute | solution.py:35
  284.1 9.7 %collective-permute-start.25 = (bf16[144,1024]{1,0:T(8,128)(2,1)S(1)}, bf16[144,1024]{1,0:T(8,128)(2,1)S(1)}, u32[]{:S(2)}, u32[]{:S(2)}) collective-permute-start(bf16[144,1024]{1,0:T(8,128)(2,1)S(1)} %get-tuple-element.30), channel_id=1, source_target_pairs={{0,4},{1,5},{2,6},{3,7},{4,8},{5,9},{6,10},{7,11},{8,12},{9,13},{1... | collective-permute-start | bytes 884744 | tf_op jit(solution)/shard_map/ppermute | solution.py:35
  284.1 14.8 %collective-permute-start.26 = (bf16[144,1024]{1,0:T(8,128)(2,1)S(1)}, bf16[144,1024]{1,0:T(8,128)(2,1)S(1)}, u32[]{:S(2)}, u32[]{:S(2)}) collective-permute-start(bf16[144,1024]{1,0:T(8,128)(2,1)S(1)} %get-tuple-element.30), channel_id=1, source_target_pairs={{0,12},{1,13},{2,14},{3,15},{4,0},{5,1},{6,2},{7,3},{8,4},{9,5},{1... | collective-permute-start | bytes 884744 | tf_op jit(solution)/shard_map/ppermute | solution.py:35
  287.7 13.2 %collective-permute-start.27 = (bf16[144,1024]{1,0:T(8,128)(2,1)S(1)}, bf16[144,1024]{1,0:T(8,128)(2,1)S(1)}, u32[]{:S(2)}, u32[]{:S(2)}) collective-permute-start(bf16[144,1024]{1,0:T(8,128)(2,1)S(1)} %get-tuple-element.30), channel_id=1, source_target_pairs={{0,8},{1,9},{2,10},{3,11},{4,12},{5,13},{6,14},{7,15},{8,0},{9,1},... | collective-permute-start | bytes 884744 | tf_op jit(solution)/shard_map/ppermute | solution.py:35
  (26 other events, 384.1 us)
